TPU v7x, 32 devices: a whole 2x2x4 slice. The times are simulated.
32 devices in a mesh: req: 16 (over z, y, x), head: 2 (over core).
Axes of the slice: x: 2, y: 2, z: 4, core: 2. Of those that a mesh axis runs over, the one named last changes fastest.
Arguments:
- tokens: bfloat16 [32, 1024], P('req'), may hold values from -6 to 6
- self_keys: bfloat16 [32, 512, 1024], P('req', None, 'head'), may hold values from -240 to 240
- self_values: bfloat16 [32, 512, 1024], P('req', None, 'head'), may hold values from -6 to 6
- self_len: int32 [32], P('req'), may hold values from 1 to 512, as said below
- cross_keys: bfloat16 [32, 512, 1024], P('req', None, 'head'), may hold values from -240 to 240
- cross_values: bfloat16 [32, 512, 1024], P('req', None, 'head'), may hold values from -6 to 6
- cross_len: int32 [32], P('req'), may hold values from 1 to 512, as said below
- give_slot: int32 [16], P('req'), may hold values from 0 to 1
- w_query: bfloat16 [1024, 1024], P(None, 'head'), may hold values from -0.1875 to 0.1875
- w_key: bfloat16 [1024, 1024], P(None, 'head'), may hold values from -0.1875 to 0.1875
- w_value: bfloat16 [1024, 1024], P(None, 'head'), may hold values from -0.1875 to 0.1875
- w_out: bfloat16 [1024, 1024], P('head'), may hold values from -0.1875 to 0.1875
- w_cross_query: bfloat16 [1024, 1024], P(None, 'head'), may hold values from -0.1875 to 0.1875
- w_cross_out: bfloat16 [1024, 1024], P('head'), may hold values from -0.1875 to 0.1875
- w_up: bfloat16 [1024, 4096], P(None, 'head'), may hold values from -0.1875 to 0.1875
- w_down: bfloat16 [4096, 1024], P('head'), may hold values from -0.09375 to 0.09375
- gain_self: float32 [1024], replicated, may hold values from 0.1 to 1.9
- gain_cross: float32 [1024], replicated, may hold values from 0.1 to 1.9
- gain_final: float32 [1024], replicated, may hold values from 0.1 to 1.9
Outputs:
- decoded: bfloat16 [32, 1024], P('req')
- new_keys: bfloat16 [32, 1024], P('req', 'head')
- new_values: bfloat16 [32, 1024], P('req', 'head')
- moved_keys: bfloat16 [16, 512, 1024], P('req', None, 'head')
- moved_values: bfloat16 [16, 512, 1024], P('req', None, 'head')
Inputs may be any that keep to these rules, and one draw needn't show every extreme that they name: `self_len`: each request fills at least one slot; some request fills all 512. `cross_len`: each request has at least one encoder position; some request has 512.
All inputs are finite; a program needn't handle non-finite values.
Results may differ from a plain program's by a relative error of at most 0.039.
Values may be sent and summed in bfloat16 or wider, within the bound.
A program may use at most 64 MiB of HBM per device.

v0:
```python
import jax
import jax.numpy as jnp
from jax import lax
from jax.sharding import PartitionSpec as P

HEAD_DIM = 64


def passed_along(block, axis, distance):
    devices = range(lax.axis_size(axis))
    route = [((i - distance) % len(devices), i) for i in devices]
    return lax.ppermute(block, axis, route)


def layer_norm(value, gain):
    mean = jnp.mean(value, axis=-1, keepdims=True)
    centred = value - mean
    spread = jnp.mean(centred * centred, axis=-1, keepdims=True)
    return centred * lax.rsqrt(spread + 1e-05) * gain


def attend(query, keys, values, lengths, fresh_key, fresh_value):
    count, span, width = keys.shape
    heads = width // HEAD_DIM
    block = min(512, span)
    query_heads = query.reshape(count, heads, HEAD_DIM)
    steps = (jnp.max(lengths) + block - 1) // block
    places = lax.iota(jnp.int32, block)

    def score_block(index, board):
        start = index * block
        piece = keys.reshape(count, block, heads, HEAD_DIM)
        scores = jnp.einsum("qhd,qshd->qhs", query_heads, piece, preferred_element_type=jnp.float32)
        valid = (start + places)[None, None, :] < lengths[:, None, None]
        scores = jnp.where(valid, scores, -jnp.inf)
        return scores

    board = lax.fori_loop(
        0, steps, score_block, jnp.full((count, heads, span), -jnp.inf, jnp.float32)
    )
    top = jnp.max(board, axis=2)
    if fresh_key is not None:
        own = jnp.sum(
            query_heads.astype(jnp.float32)
            * fresh_key.reshape(count, heads, HEAD_DIM).astype(jnp.float32),
            axis=2,
        )
        top = jnp.maximum(top, own)
    weights_all = jnp.exp(board - top[:, :, None])
    total = jnp.sum(weights_all, axis=2)

    def mix_block(index, accum):
        start = index * block
        weights = weights_all.astype(jnp.bfloat16)
        piece = values.reshape(count, block, heads, HEAD_DIM)
        return accum + jnp.einsum(
            "qhs,qshd->qhd", weights, piece, preferred_element_type=jnp.float32
        )

    mixed = lax.fori_loop(0, steps, mix_block, jnp.zeros((count, heads, HEAD_DIM), jnp.float32))
    if fresh_key is not None:
        own_weight = jnp.exp(own - top)
        total = total + own_weight
        mixed = mixed + own_weight.astype(jnp.bfloat16).astype(jnp.float32)[
            :, :, None
        ] * fresh_value.reshape(count, heads, HEAD_DIM).astype(jnp.float32)
    return (mixed / total[:, :, None]).astype(jnp.bfloat16).reshape(count, width)


def decode_layer(
    tokens, self_keys, self_values, self_len, cross_keys, cross_values, cross_len, params
):
    (
        w_query,
        w_key,
        w_value,
        w_out,
        w_cross_query,
        w_cross_out,
        w_up,
        w_down,
        gain_self,
        gain_cross,
        gain_final,
    ) = params
    scale = HEAD_DIM ** (-0.5)
    query = (jnp.dot(tokens, w_query, preferred_element_type=jnp.float32) * scale).astype(
        jnp.bfloat16
    )
    fresh_keys = jnp.dot(tokens, w_key, preferred_element_type=jnp.float32).astype(jnp.bfloat16)
    fresh_values = jnp.dot(tokens, w_value, preferred_element_type=jnp.float32).astype(jnp.bfloat16)
    self_mixed = attend(query, self_keys, self_values, self_len, fresh_keys, fresh_values)
    self_total = lax.psum(jnp.dot(self_mixed, w_out, preferred_element_type=jnp.float32), "head")
    first = layer_norm(tokens.astype(jnp.float32) + self_total, gain_self).astype(jnp.bfloat16)
    cross_query = (
        jnp.dot(first, w_cross_query, preferred_element_type=jnp.float32) * scale
    ).astype(jnp.bfloat16)
    cross_mixed = attend(cross_query, cross_keys, cross_values, cross_len, None, None)
    cross_total = lax.psum(
        jnp.dot(cross_mixed, w_cross_out, preferred_element_type=jnp.float32), "head"
    )
    second = layer_norm(first.astype(jnp.float32) + cross_total, gain_cross).astype(jnp.bfloat16)
    hidden = jax.nn.gelu(
        jnp.dot(second, w_up, preferred_element_type=jnp.float32), approximate=False
    ).astype(jnp.bfloat16)
    ffn_total = lax.psum(jnp.dot(hidden, w_down, preferred_element_type=jnp.float32), "head")
    layer_out = layer_norm(second.astype(jnp.float32) + ffn_total, gain_final).astype(jnp.bfloat16)
    return (layer_out, fresh_keys, fresh_values)


def take_slot(array, chosen):
    return lax.dynamic_slice_in_dim(array, chosen, 1, 0)


def put_slot(array, row, chosen):
    return lax.dynamic_update_slice_in_dim(array, row, chosen, 0)


def on_device(
    tokens,
    self_keys,
    self_values,
    self_len,
    cross_keys,
    cross_values,
    cross_len,
    give_slot,
    w_query,
    w_key,
    w_value,
    w_out,
    w_cross_query,
    w_cross_out,
    w_up,
    w_down,
    gain_self,
    gain_cross,
    gain_final,
):
    params = (
        w_query,
        w_key,
        w_value,
        w_out,
        w_cross_query,
        w_cross_out,
        w_up,
        w_down,
        gain_self,
        gain_cross,
        gain_final,
    )
    chosen = give_slot[0]
    half_axis = lax.axis_size("req") // 2
    moving = passed_along(
        (
            take_slot(tokens, chosen),
            take_slot(self_keys, chosen),
            take_slot(self_values, chosen),
            take_slot(cross_keys, chosen),
            take_slot(cross_values, chosen),
        ),
        "req",
        half_axis,
    )
    arrived_len = passed_along(
        (take_slot(self_len, chosen), take_slot(cross_len, chosen)), "req", half_axis
    )
    decoded, new_keys, new_values = decode_layer(
        put_slot(tokens, moving[0], chosen),
        put_slot(self_keys, moving[1], chosen),
        put_slot(self_values, moving[2], chosen),
        put_slot(self_len, arrived_len[0], chosen),
        put_slot(cross_keys, moving[3], chosen),
        put_slot(cross_values, moving[4], chosen),
        put_slot(cross_len, arrived_len[1], chosen),
        params,
    )
    moved_keys = moving[1]
    moved_values = moving[2]
    return (decoded, new_keys, new_values, moved_keys, moved_values)


def solution(mesh):
    placed = (
        P("req", None),
        P("req", None, "head"),
        P("req", None, "head"),
        P("req"),
        P("req", None, "head"),
        P("req", None, "head"),
        P("req"),
        P("req"),
        P(None, "head"),
        P(None, "head"),
        P(None, "head"),
        P("head", None),
        P(None, "head"),
        P("head", None),
        P(None, "head"),
        P("head", None),
        P(),
        P(),
        P(),
    )
    return jax.shard_map(
        on_device,
        mesh=mesh,
        in_specs=placed,
        out_specs=(
            P("req", None),
            P("req", "head"),
            P("req", "head"),
            P("req", None, "head"),
            P("req", None, "head"),
        ),
        check_vma=False,
    )
```

profile of v0, /device:TPU:0, one launch (start us, length us, event | category | flops | bytes accessed | tf_op | source)
XLA Modules:
  0.0 124.7 jit_solution(12741116588317227131)
XLA Ops:
  0.6 0.7 copy.88
  1.4 0.7 copy.87
  2.1 0.7 copy.89
  3.4 0.6 dynamic_slice.22
  4.0 4.0 %collective-permute-start.1 = (s32[1]{0:T(128)}, s32[1]{0:T(128)}, u32[]{:S(2)}, u32[]{:S(2)}) collective-permute-start(s32[1]{0:T(128)} %dynamic_slice.22), channel_id=1, source_target_pairs={{16,0},{18,2},{20,4},{22,6},{24,8},{26,10},{28,12},{30,14},{0,16},... | collective-permute-start | bytes 20 | tf_op jit(solution)/shard_map/ppermute | solution.py:12
  8.1 1.5 %copy.25 = bf16[2,512,512]{1,2,0:T(8,128)(2,1)S(1)} copy(bf16[2,512,512]{2,1,0:T(8,128)(2,1)} %param.28) | data formatting | bytes 2097152 | tf_op args[1]
  9.6 0.9 constant_dynamic-slice_fusion.3
  10.5 2.9 %collective-permute-start.2 = (bf16[1,512,512]{1,2,0:T(8,128)(2,1)}, bf16[1,512,512]{1,2,0:T(8,128)(2,1)}, u32[]{:S(2)}, u32[]{:S(2)}) collective-permute-start(bf16[1,512,512]{1,2,0:T(8,128)(2,1)} %constant_dynamic-slice_fusion.3), channel_id=1, source_target_pairs={{16,0},{18,2},{20,4},{22,6},{24,8},{26,10},{28,12},{30,14},{0,16},... | collective-permute-start | bytes 1572872 | tf_op jit(solution)/shard_map/ppermute | solution.py:12
  13.4 1.5 %copy.27 = bf16[2,512,512]{1,2,0:T(8,128)(2,1)S(1)} copy(bf16[2,512,512]{2,1,0:T(8,128)(2,1)} %param.29) | data formatting | bytes 2097152 | tf_op args[2]
  14.9 0.9 constant_dynamic-slice_fusion.2
  15.8 0.3 copy-done.2
  16.1 1.5 %copy.29 = bf16[2,512,512]{1,2,0:T(8,128)(2,1)S(1)} copy(bf16[2,512,512]{2,1,0:T(8,128)(2,1)} %param.31) | data formatting | bytes 2097152 | tf_op args[4]
  17.6 0.9 constant_dynamic-slice_fusion.1
  18.4 2.9 %collective-permute-start.5 = (bf16[1,512,512]{1,2,0:T(8,128)(2,1)}, bf16[1,512,512]{1,2,0:T(8,128)(2,1)}, u32[]{:S(2)}, u32[]{:S(2)}) collective-permute-start(bf16[1,512,512]{1,2,0:T(8,128)(2,1)} %constant_dynamic-slice_fusion.1), channel_id=1, source_target_pairs={{16,0},{18,2},{20,4},{22,6},{24,8},{26,10},{28,12},{30,14},{0,16},... | collective-permute-start | bytes 1572872 | tf_op jit(solution)/shard_map/ppermute | solution.py:12
  21.3 0.6 dynamic_slice.25
  21.9 2.3 %copy.31 = bf16[2,512,512]{1,2,0:T(8,128)(2,1)} copy(bf16[2,512,512]{2,1,0:T(8,128)(2,1)} %param.32) | data formatting | bytes 2097152 | tf_op args[5]
  24.2 1.9 %constant_dynamic-slice_fusion = bf16[1,512,512]{1,2,0:T(8,128)(2,1)} fusion(bf16[2,512,512]{1,2,0:T(8,128)(2,1)} %copy.31, s32[]{:T(128)S(6)} %select_n.35), kind=kLoop, calls=%fused_computation.84 | loop fusion | bytes 1048580 | tf_op jit(solution)/shard_map/dynamic_slice | solution.py:112
  26.1 0.7 dynamic_update_slice.22
  26.8 0.6 reduce_max.36
  28.1 53.2 %collective-permute-done.4 = s32[1]{0:T(128)} collective-permute-done((s32[1]{0:T(128)}, s32[1]{0:T(128)}, u32[]{:S(2)}, u32[]{:S(2)}) %collective-permute-start.4) | collective-permute-done | bytes 36 | tf_op jit(solution)/shard_map/ppermute | solution.py:12
  81.3 0.7 dynamic_update_slice.25
  82.0 0.6 reduce_max.38
  83.4 1.5 %fusion.7 = bf16[2,512]{1,0:T(2,128)(2,1)S(1)} fusion(bf16[2,1024]{1,0:T(2,128)(2,1)S(1)} %dynamic_update_slice.21, bf16[1024,512]{1,0:T(8,128)(2,1)} %param.35), kind=kOutput, calls=%fused_computation.13 | convolution fusion | flops 2099200 | bytes 1054720 | tf_op jit(solution)/shard_map/dot_general | solution.py:87
  85.0 1.5 %convolution_convert_fusion.1 = bf16[2,512]{1,0:T(2,128)(2,1)S(1)} fusion(bf16[2,1024]{1,0:T(2,128)(2,1)S(1)} %dynamic_update_slice.21, bf16[1024,512]{1,0:T(8,128)(2,1)} %param.36), kind=kOutput, calls=%fused_computation.16 | convolution fusion | flops 2098176 | bytes 1054720 | tf_op jit(solution)/shard_map/dot_general | solution.py:90
  86.6 1.5 %convolution_convert_fusion = bf16[2,512]{1,0:T(2,128)(2,1)S(1)} fusion(bf16[2,1024]{1,0:T(2,128)(2,1)S(1)} %dynamic_update_slice.21, bf16[1024,512]{1,0:T(8,128)(2,1)} %param.37), kind=kOutput, calls=%fused_computation.15 | convolution fusion | flops 2098176 | bytes 1054720 | tf_op jit(solution)/shard_map/dot_general | solution.py:91
  88.2 0.1 multiply_reduce_fusion.3
  88.3 1.1 constant_dynamic-update-slice_fusion.3
  89.3 0.2 fusion.90
  89.6 0.6 broadcast.133.clone
  90.2 0.7 while.52
  90.3 0.6 broadcast_select_fusion.4
  90.9 0.8 reduce_max.37
  91.8 0.9 fusion.13
  92.7 1.9 %constant_dynamic-update-slice_fusion.2 = bf16[2,512,512]{1,2,0:T(8,128)(2,1)} fusion(bf16[2,512,512]{1,2,0:T(8,128)(2,1)} %copy-done.2, bf16[1,512,512]{1,2,0:T(8,128)(2,1)} %collective-permute-done.3, s32[]{:T(128)S(6)} %select_n.35), kind=kLoop, calls=%fused_computation.87 | loop fusion | bytes 1048580 | tf_op jit(solution)/shard_map/dynamic_update_slice | solution.py:116
  94.6 1.6 %fusion.11 = f32[2,8,1,64]{3,2,1,0:T(1,128)S(1)} fusion(bf16[2,512,8,64]{1,3,2,0:T(8,128)(2,1)} %bitcast.47, bf16[2,8,512,1]{2,1,0,3:T(8,128)(2,1)S(1)} %get-tuple-element.361), kind=kOutput, calls=%fused_computation.20 | convolution fusion | flops 1048576 | bytes 1069056 | tf_op jit(solution)/shard_map/while/body/qhs,qshd->qhd/dot_general | solution.py:56
  96.2 0.1 divide_convert_fusion.1
  96.3 0.1 reshape.180
  96.4 0.3 fusion.91
  96.6 2.5 %psum.21 = f32[2,1024]{1,0:T(2,128)S(1)} all-reduce(f32[2,1024]{1,0:T(2,128)S(1)} %fusion.91), channel_id=1, replica_groups=mesh['req'=16,'head'=2] {'head'}, use_global_device_ids=true, to_apply=%region_8.9 | all-reduce | flops 2048 | bytes 16384 | tf_op jit(solution)/shard_map/psum | solution.py:93
  99.1 0.1 fusion.53
  99.2 0.2 multiply_reduce_fusion.2
  99.5 1.5 %fusion.8 = bf16[2,512]{1,0:T(2,128)(2,1)S(1)} fusion(bf16[2,1024]{1,0:T(2,128)(2,1)S(1)} %multiply_convert_fusion.2, bf16[1024,512]{1,0:T(8,128)(2,1)} %param.39), kind=kOutput, calls=%fused_computation.14 | convolution fusion | flops 2099200 | bytes 1054720 | tf_op jit(solution)/shard_map/dot_general | solution.py:96
  101.0 0.1 reshape.198
  101.1 1.1 constant_dynamic-update-slice_fusion.1
  102.2 0.2 fusion.92
  102.4 0.6 broadcast.133
  103.0 0.7 while.53
  103.1 0.6 broadcast_select_fusion.5
  103.8 0.9 fusion.6
  104.7 0.1 fusion.87
  104.8 1.7 %collective-permute-done.6 = bf16[1,512,512]{1,2,0:T(8,128)(2,1)} collective-permute-done((bf16[1,512,512]{1,2,0:T(8,128)(2,1)}, bf16[1,512,512]{1,2,0:T(8,128)(2,1)}, u32[]{:S(2)}, u32[]{:S(2)}) %collective-permute-start.6) | collective-permute-done | bytes 524320 | tf_op jit(solution)/shard_map/ppermute | solution.py:12
  106.4 1.1 constant_dynamic-update-slice_fusion
  107.5 0.4 fusion.9
  108.1 1.5 %fusion.93 = f32[2,1024]{1,0:T(2,128)S(1)} fusion(bf16[2,512]{1,0:T(2,128)(2,1)S(1)} %reshape.184, bf16[512,1024]{1,0:T(8,128)(2,1)} %param.40), kind=kOutput, calls=%fused_computation.139 | convolution fusion | flops 2097152 | bytes 1058816 | tf_op jit(solution)/shard_map/dot_general | solution.py:100
  109.6 2.5 %psum.22 = f32[2,1024]{1,0:T(2,128)S(1)} all-reduce(f32[2,1024]{1,0:T(2,128)S(1)} %fusion.93), channel_id=1, replica_groups=mesh['req'=16,'head'=2] {'head'}, use_global_device_ids=true, to_apply=%region_18.19 | all-reduce | flops 2048 | bytes 16384 | tf_op jit(solution)/shard_map/psum | solution.py:99
  112.0 0.1 fusion.54
  112.2 0.2 multiply_reduce_fusion.1
  112.4 4.7 %fusion.21 = f32[2,1024]{1,0:T(2,128)S(1)} fusion(bf16[2048,1024]{1,0:T(8,128)(2,1)} %param.42, bf16[2,1024]{1,0:T(2,128)(2,1)S(1)} %multiply_convert_fusion.1, bf16[1024,2048]{1,0:T(8,128)(2,1)} %param.41), kind=kOutput, calls=%fused_computation.40 | convolution fusion | flops 17043456 | bytes 8400896 | tf_op jit(solution)/shard_map/dot_general | solution.py:106
  117.1 2.5 %psum.23 = f32[2,1024]{1,0:T(2,128)S(1)} all-reduce(f32[2,1024]{1,0:T(2,128)S(1)} %fusion.21), channel_id=1, replica_groups=mesh['req'=16,'head'=2] {'head'}, use_global_device_ids=true, to_apply=%region_21.22 | all-reduce | flops 2048 | bytes 16384 | tf_op jit(solution)/shard_map/psum | solution.py:106
  119.6 0.1 fusion.55
  119.7 0.2 multiply_reduce_fusion
  119.9 0.7 multiply_convert_fusion
  120.6 2.0 %copy.32 = bf16[1,512,512]{2,1,0:T(8,128)(2,1)} copy(bf16[1,512,512]{1,2,0:T(8,128)(2,1)} %collective-permute-done.2) | data formatting | bytes 1048576
  122.6 2.0 %copy.33 = bf16[1,512,512]{2,1,0:T(8,128)(2,1)} copy(bf16[1,512,512]{1,2,0:T(8,128)(2,1)} %collective-permute-done.3) | data formatting | bytes 1048576
  (54 shorter events, 1.1 us)
Async XLA Ops:
  0.6 95.7 %copy-start = (bf16[512,1024]{1,0:T(8,128)(2,1)S(1)}, bf16[512,1024]{1,0:T(8,128)(2,1)}, u32[]{:S(2)}) copy-start(bf16[512,1024]{1,0:T(8,128)(2,1)} %param.38) | copy-start | bytes 3145732
  4.0 22.1 %collective-permute-start.1 = (s32[1]{0:T(128)}, s32[1]{0:T(128)}, u32[]{:S(2)}, u32[]{:S(2)}) collective-permute-start(s32[1]{0:T(128)} %dynamic_slice.22), channel_id=1, source_target_pairs={{16,0},{18,2},{20,4},{22,6},{24,8},{26,10},{28,12},{30,14},{0,16},... | collective-permute-start | bytes 20 | tf_op jit(solution)/shard_map/ppermute | solution.py:12
  8.0 75.3 %collective-permute-start = (bf16[1,1024]{1,0:T(2,128)(2,1)S(1)}, bf16[1,1024]{1,0:T(2,128)(2,1)S(1)}, u32[]{:S(2)}, u32[]{:S(2)}) collective-permute-start(bf16[1,1024]{1,0:T(2,128)(2,1)S(1)} %constant_dynamic-slice_fusion.4), channel_id=1, source_target_pairs={{16,0},{18,2},{20,4},{22,6},{24,8},{26,10},{28,12},{30,14},{0,16},... | collective-permute-start | bytes 6152 | tf_op jit(solution)/shard_map/ppermute | solution.py:12
  10.5 77.8 %collective-permute-start.2 = (bf16[1,512,512]{1,2,0:T(8,128)(2,1)}, bf16[1,512,512]{1,2,0:T(8,128)(2,1)}, u32[]{:S(2)}, u32[]{:S(2)}) collective-permute-start(bf16[1,512,512]{1,2,0:T(8,128)(2,1)} %constant_dynamic-slice_fusion.3), channel_id=1, source_target_pairs={{16,0},{18,2},{20,4},{22,6},{24,8},{26,10},{28,12},{30,14},{0,16},... | collective-permute-start | bytes 1572872 | tf_op jit(solution)/shard_map/ppermute | solution.py:12
  14.9 1.2 copy-start.2
  16.1 76.6 %collective-permute-start.3 = (bf16[1,512,512]{1,2,0:T(8,128)(2,1)}, bf16[1,512,512]{1,2,0:T(8,128)(2,1)}, u32[]{:S(2)}, u32[]{:S(2)}) collective-permute-start(bf16[1,512,512]{1,2,0:T(8,128)(2,1)} %constant_dynamic-slice_fusion.2), channel_id=1, source_target_pairs={{16,0},{18,2},{20,4},{22,6},{24,8},{26,10},{28,12},{30,14},{0,16},... | collective-permute-start | bytes 1572872 | tf_op jit(solution)/shard_map/ppermute | solution.py:12
  18.4 82.6 %collective-permute-start.5 = (bf16[1,512,512]{1,2,0:T(8,128)(2,1)}, bf16[1,512,512]{1,2,0:T(8,128)(2,1)}, u32[]{:S(2)}, u32[]{:S(2)}) collective-permute-start(bf16[1,512,512]{1,2,0:T(8,128)(2,1)} %constant_dynamic-slice_fusion.1), channel_id=1, source_target_pairs={{16,0},{18,2},{20,4},{22,6},{24,8},{26,10},{28,12},{30,14},{0,16},... | collective-permute-start | bytes 1572872 | tf_op jit(solution)/shard_map/ppermute | solution.py:12
  26.1 55.2 %collective-permute-start.4 = (s32[1]{0:T(128)}, s32[1]{0:T(128)}, u32[]{:S(2)}, u32[]{:S(2)}) collective-permute-start(s32[1]{0:T(128)} %dynamic_slice.25), channel_id=1, source_target_pairs={{16,0},{18,2},{20,4},{22,6},{24,8},{26,10},{28,12},{30,14},{0,16},... | collective-permute-start | bytes 20 | tf_op jit(solution)/shard_map/ppermute | solution.py:12
  81.3 25.1 %collective-permute-start.6 = (bf16[1,512,512]{1,2,0:T(8,128)(2,1)}, bf16[1,512,512]{1,2,0:T(8,128)(2,1)}, u32[]{:S(2)}, u32[]{:S(2)}) collective-permute-start(bf16[1,512,512]{1,2,0:T(8,128)(2,1)} %constant_dynamic-slice_fusion), channel_id=1, source_target_pairs={{16,0},{18,2},{20,4},{22,6},{24,8},{26,10},{28,12},{30,14},{0,16},... | collective-permute-start | bytes 1572872 | tf_op jit(solution)/shard_map/ppermute | solution.py:12
  85.0 14.4 %copy-start.5 = (f32[1024]{0:T(1024)S(1)}, f32[1024]{0:T(1024)}, u32[]{:S(2)}) copy-start(f32[1024]{0:T(1024)} %param.43) | copy-start | bytes 12292
  86.5 14.4 %copy-start.3 = (bf16[2,512]{1,0:T(2,128)(2,1)}, bf16[2,512]{1,0:T(2,128)(2,1)S(1)}, u32[]{:S(2)}) copy-start(bf16[2,512]{1,0:T(2,128)(2,1)S(1)} %convolution_convert_fusion.1) | copy-start | bytes 6148
  88.1 14.1 %copy-start.4 = (bf16[2,512]{1,0:T(2,128)(2,1)}, bf16[2,512]{1,0:T(2,128)(2,1)S(1)}, u32[]{:S(2)}) copy-start(bf16[2,512]{1,0:T(2,128)(2,1)S(1)} %convolution_convert_fusion) | copy-start | bytes 6148
  89.6 16.9 %copy-start.1 = (bf16[2,512,512]{1,2,0:T(8,128)(2,1)S(1)}, bf16[2,512,512]{1,2,0:T(8,128)(2,1)}, u32[]{:S(2)}) copy-start(bf16[2,512,512]{1,2,0:T(8,128)(2,1)} %copy.31) | copy-start | bytes 3145732
  96.4 16.0 %copy-start.6 = (f32[1024]{0:T(1024)S(1)}, f32[1024]{0:T(1024)}, u32[]{:S(2)}) copy-start(f32[1024]{0:T(1024)} %param.44) | copy-start | bytes 12292
  112.4 7.5 %copy-start.7 = (f32[1024]{0:T(1024)S(1)}, f32[1024]{0:T(1024)}, u32[]{:S(2)}) copy-start(f32[1024]{0:T(1024)} %param.45) | copy-start | bytes 12292
where the time goes:
time: 126 us; the launch traced here: 125 us
  waiting for transfers between devices  54.9 us (44%)
  local copies, waits for them, and re-layouts  27.4 us (22%)
  matrix products  14.7 us (12%)
  starting transfers between devices  9.96 us (8%)
  other arithmetic  7.55 us (6%)
  blocking collectives  7.39 us (6%)
  between operations  2.79 us (2%)
    ppermute x7, waiting for transfers between devices, passed_along(): return lax.ppermute(block, axis, route)  54.9 us
    unnamed x25, local copies, waits for them, and re-layouts  13.2 us
    ppermute x7, starting transfers between devices, passed_along(): return lax.ppermute(block, axis, route)  9.96 us
    dynamic_update_slice x7, local copies, waits for them, and re-layouts, put_slot(): return lax.dynamic_update_slice_in_dim(array, row, chosen, 0)  6.62 us
    dynamic_slice x7, local copies, waits for them, and re-layouts, take_slot(): return lax.dynamic_slice_in_dim(array, chosen, 1, 0)  5.67 us
    dot_general x1, matrix products, decode_layer(): jnp.dot(hidden, w_down, preferred_element_type=jnp.float32)  4.67 us
  transfers between devices with their start and end apart: 7, of which 2 were waited for; matrix products, arithmetic and copies ran while one was open for 27% of the time, Pallas kernels for 0%

commit v1 on v0

--- a/solution.py
+++ b/solution.py
@@ -152,32 +152,24 @@
     )
     chosen = give_slot[0]
     half_axis = lax.axis_size("req") // 2
-    moving = passed_along(
+    moved_keys, moved_values = passed_along(
+        (take_slot(self_keys, chosen), take_slot(self_values, chosen)), "req", half_axis
+    )
+    layer_out, fresh_keys, fresh_values = decode_layer(
+        tokens, self_keys, self_values, self_len, cross_keys, cross_values, cross_len, params
+    )
+    rows = passed_along(
         (
-            take_slot(tokens, chosen),
-            take_slot(self_keys, chosen),
-            take_slot(self_values, chosen),
-            take_slot(cross_keys, chosen),
-            take_slot(cross_values, chosen),
+            take_slot(layer_out, chosen),
+            take_slot(fresh_keys, chosen),
+            take_slot(fresh_values, chosen),
         ),
         "req",
         half_axis,
     )
-    arrived_len = passed_along(
-        (take_slot(self_len, chosen), take_slot(cross_len, chosen)), "req", half_axis
-    )
-    decoded, new_keys, new_values = decode_layer(
-        put_slot(tokens, moving[0], chosen),
-        put_slot(self_keys, moving[1], chosen),
-        put_slot(self_values, moving[2], chosen),
-        put_slot(self_len, arrived_len[0], chosen),
-        put_slot(cross_keys, moving[3], chosen),
-        put_slot(cross_values, moving[4], chosen),
-        put_slot(cross_len, arrived_len[1], chosen),
-        params,
-    )
-    moved_keys = moving[1]
-    moved_values = moving[2]
+    decoded = put_slot(layer_out, rows[0], chosen)
+    new_keys = put_slot(fresh_keys, rows[1], chosen)
+    new_values = put_slot(fresh_values, rows[2], chosen)
     return (decoded, new_keys, new_values, moved_keys, moved_values)
 
 

time: 126 us -> 58.3 us (0.46)
  waiting for transfers between devices: 54.9 us -> 2.89 us
  local copies, waits for them, and re-layouts: 27.4 us -> 14.4 us
  matrix products: 14.7 us -> 12.3 us
    ppermute x7 -> x5, waiting for transfers between devices: 54.9 us -> 2.89 us  [passed_along(): return lax.ppermute(block, axis, route)]
    dynamic_update_slice x7 -> x3, local copies, waits for them, and re-layouts: 6.62 us -> 0.13 us  [put_slot(): return lax.dynamic_update_slice_in_dim(array, row, chosen, 0)]
    unnamed x25 -> x34, local copies, waits for them, and re-layouts: 13.2 us -> 8.69 us
    dynamic_slice x7 -> x5, local copies, waits for them, and re-layouts: 5.67 us -> 3.77 us  [take_slot(): return lax.dynamic_slice_in_dim(array, chosen, 1, 0)]
    ppermute x7 -> x5, starting transfers between devices: 9.96 us -> 9.95 us  [passed_along(): return lax.ppermute(block, axis, route)]
  transfers between devices with their start and end apart: 7 -> 5, of which waited for: 2 -> 1; matrix products, arithmetic and copies ran while one was open for 27% -> 50% of each run, Pallas kernels for 0% -> 0%
where the time goes in v1:
time: 58.3 us; the launch traced here: 57.5 us
  local copies, waits for them, and re-layouts  14.4 us (25%)
  matrix products  12.3 us (21%)
  starting transfers between devices  9.95 us (17%)
  other arithmetic  7.61 us (13%)
  blocking collectives  7.39 us (13%)
  between operations  3 us (5%)
  waiting for transfers between devices  2.89 us (5%)
    ppermute x5, starting transfers between devices, passed_along(): return lax.ppermute(block, axis, route)  9.95 us
    unnamed x34, local copies, waits for them, and re-layouts  8.69 us
    dot_general x1, matrix products, decode_layer(): jnp.dot(hidden, w_down, preferred_element_type=jnp.float32)  4.67 us
    dynamic_slice x5, local copies, waits for them, and re-layouts, take_slot(): return lax.dynamic_slice_in_dim(array, chosen, 1, 0)  3.77 us
    ppermute x5, waiting for transfers between devices, passed_along(): return lax.ppermute(block, axis, route)  2.89 us
    psum x1, blocking collectives, decode_layer(): lax.psum(jnp.dot(hidden, w_down, preferred_element_type=jnp.float32), 'he...  2.47 us
    psum x1, blocking collectives, decode_layer(): lax.psum(jnp.dot(self_mixed, w_out, preferred_element_type=jnp.float32),...  2.46 us
    psum x1, blocking collectives, decode_layer(): lax.psum(jnp.dot(cross_mixed, w_cross_out, preferred_element_type=jnp.flo...  2.46 us
  transfers between devices with their start and end apart: 5, of which 1 were waited for; matrix products, arithmetic and copies ran while one was open for 50% of the time, Pallas kernels for 0%

profile of v1, /device:TPU:0, one launch (start us, length us, event | category | flops | bytes accessed | tf_op | source)
XLA Modules:
  0.0 57.5 jit_solution(13060801044764605365)
XLA Ops:
  0.6 0.0 copy-start
  0.6 0.0 copy-start.1
  1.5 0.0 copy-start.9
  1.5 1.9 %constant_dynamic-slice_fusion.1 = bf16[1,512,512]{2,1,0:T(8,128)(2,1)} fusion(bf16[2,512,512]{2,1,0:T(8,128)(2,1)} %param.28, s32[]{:T(128)S(6)} %select_n.31), kind=kLoop, calls=%fused_computation.84 | loop fusion | bytes 1048580 | tf_op jit(solution)/shard_map/dynamic_slice | solution.py:112
  3.4 4.0 %collective-permute-start.3 = (bf16[1,512,512]{2,1,0:T(8,128)(2,1)}, bf16[1,512,512]{2,1,0:T(8,128)(2,1)}, u32[]{:S(2)}, u32[]{:S(2)}) collective-permute-start(bf16[1,512,512]{2,1,0:T(8,128)(2,1)} %constant_dynamic-slice_fusion.1), channel_id=1, source_target_pairs={{16,0},{18,2},{20,4},{22,6},{24,8},{26,10},{28,12},{30,14},{0,16},... | collective-permute-start | bytes 1572872 | tf_op jit(solution)/shard_map/ppermute | solution.py:12
  7.4 1.9 %constant_dynamic-slice_fusion = bf16[1,512,512]{2,1,0:T(8,128)(2,1)} fusion(bf16[2,512,512]{2,1,0:T(8,128)(2,1)} %param.29, s32[]{:T(128)S(6)} %select_n.31), kind=kLoop, calls=%fused_computation.83 | loop fusion | bytes 1048580 | tf_op jit(solution)/shard_map/dynamic_slice | solution.py:112
  9.3 1.3 %reduce_max.36 = s32[]{:T(128)} reduce(s32[2]{0:T(128)} %param.30, s32[]{:T(128)} %constant.107.clone.1), dimensions={0}, to_apply=%region_0.0 | reduce | flops 1 | bytes 16 | tf_op jit(solution)/shard_map/reduce_max | solution.py:27
  11.2 1.5 %copy.24 = bf16[2,512,512]{1,2,0:T(8,128)(2,1)S(1)} copy(bf16[2,512,512]{2,1,0:T(8,128)(2,1)} %param.28) | data formatting | bytes 2097152 | tf_op args[1]
  12.7 1.5 %fusion.7 = bf16[2,512]{1,0:T(2,128)(2,1)S(1)} fusion(bf16[2,1024]{1,0:T(2,128)(2,1)S(1)} %copy-done.5, bf16[1024,512]{1,0:T(8,128)(2,1)} %param.35), kind=kOutput, calls=%fused_computation.13 | convolution fusion | flops 2099200 | bytes 1054720 | tf_op jit(solution)/shard_map/dot_general | solution.py:87
  14.2 0.1 reshape.196
  14.3 0.1 reshape.177
  14.4 1.3 %copy.25 = bf16[2,512,512]{1,2,0:T(8,128)(2,1)} copy(bf16[2,512,512]{2,1,0:T(8,128)(2,1)S(1)} %copy-done.1) | data formatting | bytes 2097152 | tf_op args[2]
  15.7 0.6 %reduce_max.38 = s32[]{:T(128)} reduce(s32[2]{0:T(128)S(1)} %copy-done.10, s32[]{:T(128)} %constant.107.clone.1), dimensions={0}, to_apply=%region_11.12 | reduce | flops 1 | bytes 16 | tf_op jit(solution)/shard_map/reduce_max | solution.py:27
  17.0 0.2 fusion.90
  17.3 0.6 %broadcast.133.clone = f32[2,8,512]{2,1,0:T(8,128)} broadcast(f32[]{:T(128)} %constant.112.clone.1), dimensions={} | broadcast | bytes 32772 | tf_op jit(solution)/shard_map/broadcast.9
  17.9 0.7 %while.52 = (s32[]{:T(128)}, f32[2,8,512]{2,1,0:T(8,128)}, s32[]{:T(128)}, s32[2]{0:T(128)S(1)}, f32[2,8,512]{2,1,0:T(8,128)S(1)}, /*index=5*/s32[]{:T(128)}, s32[]{:T(128)}) while((s32[]{:T(128)}, f32[2,8,512]{2,1,0:T(8,128)}, s32[]{:T(128)}, s32[2]{0:T(128)S(1)}, f32[2,8,512]{2,1,0:T(8,128)S(1)}, /*index=5*/s32[]{:T(128)}, ...), condition=%wide.region_2.3_spmd.clone, body=%wide.region_1.2_spmd.clone.sunk | while | flops 9731 | bytes 71781 | solution.py:38
  17.9 0.1 broadcast_compare_fusion.4
  18.0 0.6 %broadcast_select_fusion.4 = f32[2,8,512]{2,1,0:T(8,128)} fusion(f32[2,8,512]{2,1,0:T(8,128)S(1)} %get-tuple-element.489, pred[2,512]{1,0:T(4,128)(4,1)S(1)} %broadcast_compare_fusion.4), kind=kLoop, calls=%fused_computation.2.clone.1 | loop fusion | flops 8192 | bytes 66560 | tf_op jit(solution)/shard_map/while/body/jit(_where)/select_n | solution.py:35
  18.6 1.5 %convolution_convert_fusion.1 = bf16[2,512]{1,0:T(2,128)(2,1)S(1)} fusion(bf16[2,1024]{1,0:T(2,128)(2,1)S(1)} %copy-done.5, bf16[1024,512]{1,0:T(8,128)(2,1)} %param.36), kind=kOutput, calls=%fused_computation.16 | convolution fusion | flops 2098176 | bytes 1054720 | tf_op jit(solution)/shard_map/dot_general | solution.py:90
  20.1 0.1 reshape.185
  20.1 0.9 %reduce_max.37 = f32[2,8]{1,0:T(2,128)S(1)} reduce(f32[2,8,512]{2,1,0:T(8,128)} %get-tuple-element.289, f32[]{:T(128)} %constant.112.clone.1), dimensions={2}, to_apply=%region_3.4 | reduce | flops 8176 | bytes 32836 | tf_op jit(solution)/shard_map/reduce_max | solution.py:41
  21.0 0.1 multiply_reduce_fusion.3
  21.1 0.9 %fusion.13 = (f32[2,8]{1,0:T(2,128)S(1)}, bf16[2,8,512,1]{2,1,0,3:T(8,128)(2,1)S(1)}) fusion(f32[2,8,512]{2,1,0:T(8,128)} %get-tuple-element.289, f32[2,8]{1,0:T(2,128)S(1)} %get-tuple-element.354), kind=kLoop, calls=%fused_computation.28 | loop fusion | flops 24560 | bytes 49280 | tf_op jit(solution)/shard_map/reduce_sum | solution.py:50
  22.0 1.6 %fusion.11 = f32[2,8,1,64]{3,2,1,0:T(1,128)S(1)} fusion(bf16[2,512,8,64]{1,3,2,0:T(8,128)(2,1)} %bitcast.48, bf16[2,8,512,1]{2,1,0,3:T(8,128)(2,1)S(1)} %get-tuple-element.356), kind=kOutput, calls=%fused_computation.20 | convolution fusion | flops 1048576 | bytes 1069056 | tf_op jit(solution)/shard_map/while/body/qhs,qshd->qhd/dot_general | solution.py:56
  23.6 1.5 %convolution_convert_fusion = bf16[2,512]{1,0:T(2,128)(2,1)S(1)} fusion(bf16[2,1024]{1,0:T(2,128)(2,1)S(1)} %copy-done.5, bf16[1024,512]{1,0:T(8,128)(2,1)} %param.37), kind=kOutput, calls=%fused_computation.15 | convolution fusion | flops 2098176 | bytes 1054720 | tf_op jit(solution)/shard_map/dot_general | solution.py:91
  25.1 0.1 reshape.186
  25.2 0.1 divide_convert_fusion.1
  25.3 0.1 reshape.180
  25.4 0.3 fusion.91
  25.6 2.5 %psum.21 = f32[2,1024]{1,0:T(2,128)S(1)} all-reduce(f32[2,1024]{1,0:T(2,128)S(1)} %fusion.91), channel_id=1, replica_groups=mesh['req'=16,'head'=2] {'head'}, use_global_device_ids=true, to_apply=%region_8.9 | all-reduce | flops 2048 | bytes 16384 | tf_op jit(solution)/shard_map/psum | solution.py:93
  28.1 0.1 fusion.53
  28.2 0.2 multiply_reduce_fusion.2
  28.4 0.1 multiply_convert_fusion.2
  28.5 0.2 fusion.8
  28.8 0.1 reshape.198
  28.9 0.6 copy.26
  29.4 0.2 fusion.92
  29.7 0.6 %broadcast.133 = f32[2,8,512]{2,1,0:T(8,128)} broadcast(f32[]{:T(128)} %constant.112.clone.1), dimensions={} | broadcast | bytes 32772 | tf_op jit(solution)/shard_map/broadcast.9
  30.3 0.7 %while.53 = (s32[]{:T(128)}, f32[2,8,512]{2,1,0:T(8,128)}, s32[]{:T(128)}, s32[2]{0:T(128)S(1)}, f32[2,8,512]{2,1,0:T(8,128)S(1)}, /*index=5*/s32[]{:T(128)}, s32[]{:T(128)}) while((s32[]{:T(128)}, f32[2,8,512]{2,1,0:T(8,128)}, s32[]{:T(128)}, s32[2]{0:T(128)S(1)}, f32[2,8,512]{2,1,0:T(8,128)S(1)}, /*index=5*/s32[]{:T(128)}, ...), condition=%wide.region_13.14_spmd.clone, body=%wide.region_12.13_spmd.clone.sunk | while | flops 9731 | bytes 71781 | solution.py:38
  30.3 0.1 broadcast_compare_fusion.5
  30.4 0.6 %broadcast_select_fusion.5 = f32[2,8,512]{2,1,0:T(8,128)} fusion(f32[2,8,512]{2,1,0:T(8,128)S(1)} %get-tuple-element.525, pred[2,512]{1,0:T(4,128)(4,1)S(1)} %broadcast_compare_fusion.5), kind=kLoop, calls=%fused_computation.5.clone.1 | loop fusion | flops 8192 | bytes 66560 | tf_op jit(solution)/shard_map/while/body/jit(_where)/select_n | solution.py:35
  31.0 0.9 %fusion.6 = f32[2,8,512]{2,1,0:T(8,128)S(1)} fusion(f32[2,8,512]{2,1,0:T(8,128)} %get-tuple-element.291), kind=kOutput, calls=%fused_computation.10 | output fusion | flops 8719 | bytes 65536 | tf_op jit(solution)/shard_map/sub | solution.py:49
  31.9 0.1 fusion.87
  32.0 1.5 %copy.27 = bf16[2,512,512]{1,2,0:T(8,128)(2,1)S(1)} copy(bf16[2,512,512]{2,1,0:T(8,128)(2,1)} %param.32) | data formatting | bytes 2097152 | tf_op args[5]
  33.5 0.4 fusion.9
  33.9 0.1 divide_convert_fusion
  34.0 0.1 reshape.184
  34.1 0.3 fusion.93
  34.3 2.5 %psum.22 = f32[2,1024]{1,0:T(2,128)S(1)} all-reduce(f32[2,1024]{1,0:T(2,128)S(1)} %fusion.93), channel_id=1, replica_groups=mesh['req'=16,'head'=2] {'head'}, use_global_device_ids=true, to_apply=%region_18.19 | all-reduce | flops 2048 | bytes 16384 | tf_op jit(solution)/shard_map/psum | solution.py:99
  36.8 0.1 fusion.54
  36.9 0.2 multiply_reduce_fusion.1
  37.1 0.1 multiply_convert_fusion.1
  37.2 4.7 %fusion.21 = f32[2,1024]{1,0:T(2,128)S(1)} fusion(bf16[2048,1024]{1,0:T(8,128)(2,1)} %param.42, bf16[2,1024]{1,0:T(2,128)(2,1)S(1)} %multiply_convert_fusion.1, bf16[1024,2048]{1,0:T(8,128)(2,1)} %param.41), kind=kOutput, calls=%fused_computation.40 | convolution fusion | flops 17043456 | bytes 8400896 | tf_op jit(solution)/shard_map/dot_general | solution.py:106
  41.9 2.5 %psum.23 = f32[2,1024]{1,0:T(2,128)S(1)} all-reduce(f32[2,1024]{1,0:T(2,128)S(1)} %fusion.21), channel_id=1, replica_groups=mesh['req'=16,'head'=2] {'head'}, use_global_device_ids=true, to_apply=%region_21.22 | all-reduce | flops 2048 | bytes 16384 | tf_op jit(solution)/shard_map/psum | solution.py:106
  44.3 0.1 fusion.55
  44.5 0.2 multiply_reduce_fusion
  44.7 0.1 multiply_convert_fusion
  44.8 3.0 %collective-permute-start = (bf16[1,1024]{1,0:T(2,128)(2,1)S(1)}, bf16[1,1024]{1,0:T(2,128)(2,1)S(1)}, u32[]{:S(2)}, u32[]{:S(2)}) collective-permute-start(bf16[1,1024]{1,0:T(2,128)(2,1)S(1)} %constant_dynamic-slice_fusion.4), channel_id=1, source_target_pairs={{16,0},{18,2},{20,4},{22,6},{24,8},{26,10},{28,12},{30,14},{0,16},... | collective-permute-start | bytes 6152 | tf_op jit(solution)/shard_map/ppermute | solution.py:12
  47.8 0.1 collective-permute-start.1
  47.9 2.8 %collective-permute-start.2 = (bf16[1,512]{1,0:T(2,128)(2,1)S(1)}, bf16[1,512]{1,0:T(2,128)(2,1)S(1)}, u32[]{:S(2)}, u32[]{:S(2)}) collective-permute-start(bf16[1,512]{1,0:T(2,128)(2,1)S(1)} %constant_dynamic-slice_fusion.2), channel_id=1, source_target_pairs={{16,0},{18,2},{20,4},{22,6},{24,8},{26,10},{28,12},{30,14},{0,16},... | collective-permute-start | bytes 3080 | tf_op jit(solution)/shard_map/ppermute | solution.py:12
  50.7 2.9 %collective-permute-done.1 = bf16[1,512]{1,0:T(2,128)(2,1)S(1)} collective-permute-done((bf16[1,512]{1,0:T(2,128)(2,1)S(1)}, bf16[1,512]{1,0:T(2,128)(2,1)S(1)}, u32[]{:S(2)}, u32[]{:S(2)}) %collective-permute-start.1) | collective-permute-done | bytes 1056 | tf_op jit(solution)/shard_map/ppermute | solution.py:12
  53.7 0.0 copy-start.8
  53.8 1.9 %copy.75 = bf16[1,512,512]{2,1,0:T(8,128)(2,1)} copy(bf16[1,512,512]{2,1,0:T(8,128)(2,1)} %collective-permute-done.3) | data formatting | bytes 1048576
  55.6 1.9 %copy.76 = bf16[1,512,512]{2,1,0:T(8,128)(2,1)} copy(bf16[1,512,512]{2,1,0:T(8,128)(2,1)} %collective-permute-done.4) | data formatting | bytes 1048576
  (53 shorter events, 0.3 us)
Async XLA Ops:
  0.6 24.8 %copy-start = (bf16[512,1024]{1,0:T(8,128)(2,1)S(1)}, bf16[512,1024]{1,0:T(8,128)(2,1)}, u32[]{:S(2)}) copy-start(bf16[512,1024]{1,0:T(8,128)(2,1)} %param.38) | copy-start | bytes 3145732
  0.6 13.7 %copy-start.1 = (bf16[2,512,512]{2,1,0:T(8,128)(2,1)S(1)}, bf16[2,512,512]{2,1,0:T(8,128)(2,1)}, u32[]{:S(2)}) copy-start(bf16[2,512,512]{2,1,0:T(8,128)(2,1)} %param.29) | copy-start | bytes 3145732
  0.7 12.1 %copy-start.5 = (bf16[2,1024]{1,0:T(2,128)(2,1)S(1)}, bf16[2,1024]{1,0:T(2,128)(2,1)}, u32[]{:S(2)}) copy-start(bf16[2,1024]{1,0:T(2,128)(2,1)} %param.27) | copy-start | bytes 12292
  0.7 15.1 %copy-start.10 = (s32[2]{0:T(128)S(1)}, s32[2]{0:T(128)}, u32[]{:S(2)}) copy-start(s32[2]{0:T(128)} %param.33) | copy-start | bytes 28
  1.5 16.4 %copy-start.9 = (s32[2]{0:T(128)S(1)}, s32[2]{0:T(128)}, u32[]{:S(2)}) copy-start(s32[2]{0:T(128)} %param.30) | copy-start | bytes 28
  3.4 50.4 %collective-permute-start.3 = (bf16[1,512,512]{2,1,0:T(8,128)(2,1)}, bf16[1,512,512]{2,1,0:T(8,128)(2,1)}, u32[]{:S(2)}, u32[]{:S(2)}) collective-permute-start(bf16[1,512,512]{2,1,0:T(8,128)(2,1)} %constant_dynamic-slice_fusion.1), channel_id=1, source_target_pairs={{16,0},{18,2},{20,4},{22,6},{24,8},{26,10},{28,12},{30,14},{0,16},... | collective-permute-start | bytes 1572872 | tf_op jit(solution)/shard_map/ppermute | solution.py:12
  9.3 44.5 %collective-permute-start.4 = (bf16[1,512,512]{2,1,0:T(8,128)(2,1)}, bf16[1,512,512]{2,1,0:T(8,128)(2,1)}, u32[]{:S(2)}, u32[]{:S(2)}) collective-permute-start(bf16[1,512,512]{2,1,0:T(8,128)(2,1)} %constant_dynamic-slice_fusion), channel_id=1, source_target_pairs={{16,0},{18,2},{20,4},{22,6},{24,8},{26,10},{28,12},{30,14},{0,16},... | collective-permute-start | bytes 1572872 | tf_op jit(solution)/shard_map/ppermute | solution.py:12
  14.4 14.1 %copy-start.11 = (f32[1024]{0:T(1024)S(1)}, f32[1024]{0:T(1024)}, u32[]{:S(2)}) copy-start(f32[1024]{0:T(1024)} %param.43) | copy-start | bytes 12292
  17.3 11.2 %copy-start.2 = (bf16[1024,512]{1,0:T(8,128)(2,1)S(1)}, bf16[1024,512]{1,0:T(8,128)(2,1)}, u32[]{:S(2)}) copy-start(bf16[1024,512]{1,0:T(8,128)(2,1)} %param.39) | copy-start | bytes 3145732
  17.3 11.6 %copy-start.3 = (bf16[2,512,512]{2,1,0:T(8,128)(2,1)S(1)}, bf16[2,512,512]{2,1,0:T(8,128)(2,1)}, u32[]{:S(2)}) copy-start(bf16[2,512,512]{2,1,0:T(8,128)(2,1)} %param.31) | copy-start | bytes 3145732
  28.9 8.3 %copy-start.12 = (f32[1024]{0:T(1024)S(1)}, f32[1024]{0:T(1024)}, u32[]{:S(2)}) copy-start(f32[1024]{0:T(1024)} %param.44) | copy-start | bytes 12292
  29.4 4.6 %copy-start.4 = (bf16[512,1024]{1,0:T(8,128)(2,1)S(1)}, bf16[512,1024]{1,0:T(8,128)(2,1)}, u32[]{:S(2)}) copy-start(bf16[512,1024]{1,0:T(8,128)(2,1)} %param.40) | copy-start | bytes 3145732
  37.2 7.5 %copy-start.13 = (f32[1024]{0:T(1024)S(1)}, f32[1024]{0:T(1024)}, u32[]{:S(2)}) copy-start(f32[1024]{0:T(1024)} %param.45) | copy-start | bytes 12292
  44.8 8.9 %collective-permute-start = (bf16[1,1024]{1,0:T(2,128)(2,1)S(1)}, bf16[1,1024]{1,0:T(2,128)(2,1)S(1)}, u32[]{:S(2)}, u32[]{:S(2)}) collective-permute-start(bf16[1,1024]{1,0:T(2,128)(2,1)S(1)} %constant_dynamic-slice_fusion.4), channel_id=1, source_target_pairs={{16,0},{18,2},{20,4},{22,6},{24,8},{26,10},{28,12},{30,14},{0,16},... | collective-permute-start | bytes 6152 | tf_op jit(solution)/shard_map/ppermute | solution.py:12
  47.8 5.8 %collective-permute-start.1 = (bf16[1,512]{1,0:T(2,128)(2,1)S(1)}, bf16[1,512]{1,0:T(2,128)(2,1)S(1)}, u32[]{:S(2)}, u32[]{:S(2)}) collective-permute-start(bf16[1,512]{1,0:T(2,128)(2,1)S(1)} %constant_dynamic-slice_fusion.3), channel_id=1, source_target_pairs={{16,0},{18,2},{20,4},{22,6},{24,8},{26,10},{28,12},{30,14},{0,16},... | collective-permute-start | bytes 3080 | tf_op jit(solution)/shard_map/ppermute | solution.py:12
  47.9 5.8 %collective-permute-start.2 = (bf16[1,512]{1,0:T(2,128)(2,1)S(1)}, bf16[1,512]{1,0:T(2,128)(2,1)S(1)}, u32[]{:S(2)}, u32[]{:S(2)}) collective-permute-start(bf16[1,512]{1,0:T(2,128)(2,1)S(1)} %constant_dynamic-slice_fusion.2), channel_id=1, source_target_pairs={{16,0},{18,2},{20,4},{22,6},{24,8},{26,10},{28,12},{30,14},{0,16},... | collective-permute-start | bytes 3080 | tf_op jit(solution)/shard_map/ppermute | solution.py:12
  53.6 3.9 %copy-start.6 = (bf16[2,512]{1,0:T(2,128)(2,1)}, bf16[2,512]{1,0:T(2,128)(2,1)S(1)}, u32[]{:S(2)}) copy-start(bf16[2,512]{1,0:T(2,128)(2,1)S(1)} %dynamic_update_slice.10) | copy-start | bytes 6148
  53.7 3.8 %copy-start.7 = (bf16[2,512]{1,0:T(2,128)(2,1)}, bf16[2,512]{1,0:T(2,128)(2,1)S(1)}, u32[]{:S(2)}) copy-start(bf16[2,512]{1,0:T(2,128)(2,1)S(1)} %dynamic_update_slice.11) | copy-start | bytes 6148
  53.7 3.8 %copy-start.8 = (bf16[2,1024]{1,0:T(2,128)(2,1)}, bf16[2,1024]{1,0:T(2,128)(2,1)S(1)}, u32[]{:S(2)}) copy-start(bf16[2,1024]{1,0:T(2,128)(2,1)S(1)} %dynamic_update_slice.9) | copy-start | bytes 12292

commit v2 on v1

v2 whole, which is shorter than its diff:
```python
import functools

import jax
import jax.numpy as jnp
from jax import lax
from jax.experimental import pallas as pl
from jax.experimental.pallas import tpu as pltpu
from jax.sharding import PartitionSpec as P

HEAD_DIM = 64
LANES = 128
ROWS = 8
MESH = pl.DeviceIdType.MESH


def layer_norm(value, gain):
    mean = jnp.mean(value, axis=-1, keepdims=True)
    centred = value - mean
    spread = jnp.mean(centred * centred, axis=-1, keepdims=True)
    return centred * lax.rsqrt(spread + 1e-05) * gain


def rounded(value):
    return value.astype(jnp.bfloat16).astype(jnp.float32)


def project(left, right):
    return jnp.dot(left.astype(jnp.bfloat16), right, preferred_element_type=jnp.float32)


def attend_one(query, keys, values, length, fresh_key, fresh_value):
    width = query.shape[1]
    rows = max(ROWS, width // HEAD_DIM)
    head_of = lax.broadcasted_iota(jnp.int32, (rows, width), 1) // HEAD_DIM
    own_head = head_of == lax.broadcasted_iota(jnp.int32, (rows, width), 0)
    spread_query = jnp.where(own_head, query, 0.0)
    scores = lax.dot_general(
        spread_query.astype(jnp.bfloat16),
        keys,
        (((1,), (1,)), ((), ())),
        preferred_element_type=jnp.float32,
    )
    places = lax.broadcasted_iota(jnp.int32, scores.shape, 1)
    scores = jnp.where(places < length, scores, -jnp.inf)
    top = jnp.max(scores, axis=1, keepdims=True)
    if fresh_key is not None:
        own = jnp.sum(spread_query * fresh_key, axis=1, keepdims=True)
        top = jnp.maximum(top, own)
    weights = jnp.exp(scores - top)
    total = jnp.sum(weights, axis=1, keepdims=True)
    mixed = project(weights, values)
    if fresh_key is not None:
        own_weight = jnp.exp(own - top)
        total = total + own_weight
        mixed = mixed + rounded(own_weight) * fresh_value
    return jnp.sum(jnp.where(own_head, mixed / total, 0.0), axis=0, keepdims=True)


def kernel(
    parts,
    places,
    self_len,
    cross_len,
    give_slot,
    tokens,
    gain_self,
    gain_cross,
    gain_final,
    self_keys,
    self_values,
    cross_keys,
    cross_values,
    w_query,
    w_key,
    w_value,
    w_out,
    w_cross_query,
    w_cross_out,
    w_up,
    w_down,
    decoded,
    new_keys,
    new_values,
    moved_keys,
    moved_values,
    keys_in,
    values_in,
    cross_keys_in,
    cross_values_in,
    query_in,
    key_in,
    value_in,
    out_in,
    cross_query_in,
    cross_out_in,
    up_in,
    down_in,
    keys_away,
    values_away,
    hold,
    mix_hold,
    terms,
    row_away,
    row_home,
    load_sem,
    move_send,
    move_recv,
    term_send,
    term_recv,
):
    place = lax.axis_index("req")
    part = lax.axis_index("head")
    partner = lax.rem(place + places // 2, places)
    peers = [lax.rem(part + step, parts) for step in range(1, parts)]

    loads = []
    for index, (source, target) in enumerate(
        (
            (self_keys, keys_in),
            (self_values, values_in),
            (w_query, query_in),
            (w_key, key_in),
            (w_value, value_in),
            (w_out, out_in),
            (w_cross_query, cross_query_in),
            (cross_keys, cross_keys_in),
            (cross_values, cross_values_in),
            (w_cross_out, cross_out_in),
            (w_up, up_in),
            (w_down, down_in),
        )
    ):
        load = pltpu.make_async_copy(source, target, load_sem.at[index])
        load.start()
        loads.append(load)

    barrier = pltpu.get_barrier_semaphore()
    pl.semaphore_signal(barrier, inc=1, device_id=(partner, part), device_id_type=MESH)
    for peer in peers:
        pl.semaphore_signal(barrier, inc=1, device_id=(place, peer), device_id_type=MESH)

    chosen = give_slot[0]
    first_chosen = chosen == 0

    loads[0].wait()
    keys_away[...] = jnp.where(first_chosen, keys_in[0], keys_in[1])
    pl.semaphore_wait(barrier, parts)

    def send(source, target, index):
        copy = pltpu.make_async_remote_copy(
            src_ref=source,
            dst_ref=target,
            send_sem=move_send.at[index],
            recv_sem=move_recv.at[index],
            device_id=(partner, part),
            device_id_type=MESH,
        )
        copy.start()
        return copy

    keys_copy = send(keys_away, moved_keys.at[0], 0)
    loads[1].wait()
    values_away[...] = jnp.where(first_chosen, values_in[0], values_in[1])
    values_copy = send(values_away, moved_values.at[0], 1)

    def summed(phase, term):
        terms[phase, part] = term
        copies = []
        for step, peer in enumerate(peers):
            copy = pltpu.make_async_remote_copy(
                src_ref=terms.at[phase, part],
                dst_ref=terms.at[phase, part],
                send_sem=term_send.at[phase, step],
                recv_sem=term_recv.at[phase, step],
                device_id=(place, peer),
                device_id_type=MESH,
            )
            copy.start()
            copies.append(copy)
        for copy in copies:
            copy.wait()
        total = terms[phase, 0]
        for index in range(1, parts):
            total = total + terms[phase, index]
        return total

    count = tokens.shape[0]
    scale = HEAD_DIM ** (-0.5)
    hold[...] = jnp.zeros_like(hold)
    hold[0:count, :] = tokens[...].astype(jnp.float32)
    own = hold[...]
    loads[2].wait()
    query = rounded(project(own, query_in[...]) * scale)
    loads[3].wait()
    fresh_keys = rounded(project(own, key_in[...]))
    loads[4].wait()
    fresh_values = rounded(project(own, value_in[...]))

    mix_hold[...] = jnp.zeros_like(mix_hold)
    for index in range(count):
        mix_hold[index : index + 1, :] = attend_one(
            query[index : index + 1],
            keys_in[index],
            values_in[index],
            self_len[index],
            fresh_keys[index : index + 1],
            fresh_values[index : index + 1],
        )
    loads[5].wait()
    total = summed(0, project(mix_hold[...], out_in[...]))
    first = rounded(layer_norm(own + total, gain_self[...]))

    loads[6].wait()
    cross_query = rounded(project(first, cross_query_in[...]) * scale)
    loads[7].wait()
    loads[8].wait()
    for index in range(count):
        mix_hold[index : index + 1, :] = attend_one(
            cross_query[index : index + 1],
            cross_keys_in[index],
            cross_values_in[index],
            cross_len[index],
            None,
            None,
        )
    loads[9].wait()
    total = summed(1, project(mix_hold[...], cross_out_in[...]))
    second = rounded(layer_norm(first + total, gain_cross[...]))

    loads[10].wait()
    hidden = project(second, up_in[...])
    hidden = 0.5 * hidden * (1.0 + lax.erf(hidden * (0.5**0.5)))
    loads[11].wait()
    total = summed(2, project(hidden, down_in[...]))
    layer_out = rounded(layer_norm(second + total, gain_final[...]))

    results = ((layer_out, decoded), (fresh_keys, new_keys), (fresh_values, new_values))
    row_away[...] = jnp.zeros_like(row_away)
    spot = 0
    for value, _ in results:
        row = jnp.where(first_chosen, value[0:1], value[1:2])
        for piece in range(value.shape[1] // LANES):
            row_away[spot : spot + 1, :] = row[:, piece * LANES : (piece + 1) * LANES]
            spot += 1
    row_copy = send(row_away, row_home, 2)
    row_copy.wait()
    spot = 0
    for value, output in results:
        for piece in range(value.shape[1] // LANES):
            span = slice(piece * LANES, (piece + 1) * LANES)
            mine = value[0:count, span]
            slots = lax.broadcasted_iota(jnp.int32, mine.shape, 0)
            mine = jnp.where(slots == chosen, row_home[spot : spot + 1, :], mine)
            output[:, span] = mine.astype(jnp.bfloat16)
            spot += 1
    keys_copy.wait()
    values_copy.wait()


def on_device(
    tokens,
    self_keys,
    self_values,
    self_len,
    cross_keys,
    cross_values,
    cross_len,
    give_slot,
    w_query,
    w_key,
    w_value,
    w_out,
    w_cross_query,
    w_cross_out,
    w_up,
    w_down,
    gain_self,
    gain_cross,
    gain_final,
):
    parts, places = lax.axis_size("head"), lax.axis_size("req")
    count, depth = tokens.shape
    span, width = self_keys.shape[1:]
    pieces = (depth + 2 * width) // LANES
    tall = (pieces + ROWS - 1) // ROWS * ROWS
    big = (
        self_keys,
        self_values,
        cross_keys,
        cross_values,
        w_query,
        w_key,
        w_value,
        w_out,
        w_cross_query,
        w_cross_out,
        w_up,
        w_down,
    )
    whole = pl.BlockSpec(memory_space=pltpu.VMEM)
    scalars = pl.BlockSpec(memory_space=pltpu.SMEM)
    anywhere = pl.BlockSpec(memory_space=pl.ANY)
    bf16, f32 = jnp.bfloat16, jnp.float32
    size = sum(array.size for array in big)
    return pl.pallas_call(
        functools.partial(kernel, parts, places),
        out_shape=(
            jax.ShapeDtypeStruct((count, depth), bf16),
            jax.ShapeDtypeStruct((count, width), bf16),
            jax.ShapeDtypeStruct((count, width), bf16),
            jax.ShapeDtypeStruct((1, span, width), bf16),
            jax.ShapeDtypeStruct((1, span, width), bf16),
        ),
        in_specs=[scalars] * 3 + [whole] * 4 + [anywhere] * 12,
        out_specs=(whole, whole, whole, anywhere, anywhere),
        scratch_shapes=[pltpu.VMEM(array.shape, bf16) for array in big]
        + [
            pltpu.VMEM((span, width), bf16),
            pltpu.VMEM((span, width), bf16),
            pltpu.VMEM((ROWS, depth), f32),
            pltpu.VMEM((ROWS, width), f32),
            pltpu.VMEM((3, parts, ROWS, depth), f32),
            pltpu.VMEM((tall, LANES), f32),
            pltpu.VMEM((tall, LANES), f32),
            pltpu.SemaphoreType.DMA((len(big),)),
            pltpu.SemaphoreType.DMA((3,)),
            pltpu.SemaphoreType.DMA((3,)),
            pltpu.SemaphoreType.DMA((3, parts)),
            pltpu.SemaphoreType.DMA((3, parts)),
        ],
        compiler_params=pltpu.CompilerParams(
            collective_id=0, has_side_effects=True, vmem_limit_bytes=56 * 2**20
        ),
        cost_estimate=pl.CostEstimate(flops=4 * size, bytes_accessed=2 * size, transcendentals=0),
    )(
        self_len,
        cross_len,
        give_slot,
        tokens,
        gain_self.reshape(1, depth),
        gain_cross.reshape(1, depth),
        gain_final.reshape(1, depth),
        *big,
    )


def solution(mesh):
    placed = (
        P("req", None),
        P("req", None, "head"),
        P("req", None, "head"),
        P("req"),
        P("req", None, "head"),
        P("req", None, "head"),
        P("req"),
        P("req"),
        P(None, "head"),
        P(None, "head"),
        P(None, "head"),
        P("head", None),
        P(None, "head"),
        P("head", None),
        P(None, "head"),
        P("head", None),
        P(),
        P(),
        P(),
    )
    return jax.shard_map(
        on_device,
        mesh=mesh,
        in_specs=placed,
        out_specs=(
            P("req", None),
            P("req", "head"),
            P("req", "head"),
            P("req", None, "head"),
            P("req", None, "head"),
        ),
        check_vma=False,
    )
```

time: 58.3 us -> 62.1 us (1.065)
  Pallas kernels: 0 us -> 53 us
  matrix products: 12.3 us -> 0 us
  starting transfers between devices: 9.95 us -> 0 us
  other arithmetic: 7.61 us -> 0 us
  blocking collectives: 7.39 us -> 0 us
  local copies, waits for them, and re-layouts: 14.4 us -> 7.49 us
  waiting for transfers between devices: 2.89 us -> 0 us
  between operations: 3 us -> 1.29 us
    pallas_call x0 -> x1, Pallas kernels: none -> 53 us  [on_device(): pl.pallas_call(functools.partial(kernel, parts, places), out_shape=(jax.S...]
    dot_general x11 -> x0, matrix products: 12.3 us -> none  [the longest x1 4.67 us: decode_layer(): jnp.dot(hidden, w_down, preferred_element_type=jnp.float32)]
    ppermute x5 -> x0, starting transfers between devices: 9.95 us -> none  [passed_along(): return lax.ppermute(block, axis, route)]
    psum x3 -> x0, blocking collectives: 7.39 us -> none  [the longest x1 2.47 us: decode_layer(): lax.psum(jnp.dot(hidden, w_down, preferred_element_type=jnp.float32), 'he...]
    dynamic_slice x5 -> x0, local copies, waits for them, and re-layouts: 3.77 us -> none  [take_slot(): return lax.dynamic_slice_in_dim(array, chosen, 1, 0)]
    ppermute x5 -> x0, waiting for transfers between devices: 2.89 us -> none  [passed_along(): return lax.ppermute(block, axis, route)]
    reduce_max x3 -> x0, other arithmetic: 2.78 us -> none  [the longest x2 1.92 us: attend(): steps = (jnp.max(lengths) + block - 1) // block]
    reduce_sum x9 -> x0, other arithmetic: 2.05 us -> none  [the longest x2 1.02 us: attend(): total = jnp.sum(weights_all, axis=2)]
  transfers between devices with their start and end apart: 5 -> 0, of which waited for: 1 -> 0; matrix products, arithmetic and copies ran while one was open for 50% -> 0% of each run, Pallas kernels for 0% -> 0%
where the time goes in v2:
time: 62.1 us; the launch traced here: 61.8 us
  Pallas kernels  53 us (85%)
  local copies, waits for them, and re-layouts  7.49 us (12%)
  between operations  1.29 us (2%)
    pallas_call x1, Pallas kernels, on_device(): pl.pallas_call(functools.partial(kernel, parts, places), out_shape=(jax.S...  53 us
    unnamed x5, local copies, waits for them, and re-layouts  7.49 us

profile of v2, /device:TPU:0, one launch (start us, length us, event | category | flops | bytes accessed | tf_op | source)
XLA Modules:
  0.0 61.8 jit_solution(2772591672796996056)
XLA Ops:
  1.3 53.0 %shard_map.218 = (bf16[2,1024]{1,0:T(2,128)(2,1)}, bf16[2,512]{1,0:T(2,128)(2,1)}, bf16[2,512]{1,0:T(2,128)(2,1)}, bf16[1,512,512]{2,1,0:T(8,128)(2,1)}, bf16[1,512,512]{2,1,0:T(8,128)(2,1)}) custom-call(s32[2]{0:T(128)} %self_len.1, s32[2]{0:T(128)} %cross_len.1, s32[1]{0:T(128)S(6)} %copy.29.give_slot, bf16[2,1024]{1,0:T(2,128)(2,1)} %tokens.1, ...), custom_call_target="tpu_custom_call" | custom-call | flops 37748736 | bytes 18874368 | tf_op jit(solution)/shard_map/pallas_call | solution.py:305
  54.3 1.3 %copy.30 = bf16[2,1024]{1,0:T(2,128)(2,1)} copy(bf16[2,1024]{1,0:T(2,128)(2,1)} %get-tuple-element.10) | data formatting | bytes 8192
  55.6 1.2 %copy.31 = bf16[2,512]{1,0:T(2,128)(2,1)} copy(bf16[2,512]{1,0:T(2,128)(2,1)} %get-tuple-element.11) | data formatting | bytes 4096
  56.8 1.2 %copy.32 = bf16[2,512]{1,0:T(2,128)(2,1)} copy(bf16[2,512]{1,0:T(2,128)(2,1)} %get-tuple-element.12) | data formatting | bytes 4096
  58.1 1.9 %copy.33 = bf16[1,512,512]{2,1,0:T(8,128)(2,1)} copy(bf16[1,512,512]{2,1,0:T(8,128)(2,1)} %get-tuple-element.13) | data formatting | bytes 1048576
  59.9 1.9 %copy.34 = bf16[1,512,512]{2,1,0:T(8,128)(2,1)} copy(bf16[1,512,512]{2,1,0:T(8,128)(2,1)} %get-tuple-element.14) | data formatting | bytes 1048576

commit v3 on v2

--- a/solution.py
+++ b/solution.py
@@ -257,6 +257,19 @@
     values_copy.wait()
 
 
+def hand_over(*refs):
+    count = (len(refs) - 1) // 2
+    sems = refs[-1]
+    order = sorted(range(count), key=lambda index: -refs[index].size)
+    copies = [
+        pltpu.make_async_copy(refs[index], refs[count + index], sems.at[index]) for index in order
+    ]
+    for copy in copies:
+        copy.start()
+    for copy in copies:
+        copy.wait()
+
+
 def on_device(
     tokens,
     self_keys,
@@ -302,17 +315,17 @@
     anywhere = pl.BlockSpec(memory_space=pl.ANY)
     bf16, f32 = jnp.bfloat16, jnp.float32
     size = sum(array.size for array in big)
-    return pl.pallas_call(
+    results = pl.pallas_call(
         functools.partial(kernel, parts, places),
         out_shape=(
-            jax.ShapeDtypeStruct((count, depth), bf16),
-            jax.ShapeDtypeStruct((count, width), bf16),
-            jax.ShapeDtypeStruct((count, width), bf16),
-            jax.ShapeDtypeStruct((1, span, width), bf16),
-            jax.ShapeDtypeStruct((1, span, width), bf16),
+            pltpu.VMEM((count, depth), bf16),
+            pltpu.VMEM((count, width), bf16),
+            pltpu.VMEM((count, width), bf16),
+            pltpu.VMEM((1, span, width), bf16),
+            pltpu.VMEM((1, span, width), bf16),
         ),
         in_specs=[scalars] * 3 + [whole] * 4 + [anywhere] * 12,
-        out_specs=(whole, whole, whole, anywhere, anywhere),
+        out_specs=(whole,) * 5,
         scratch_shapes=[pltpu.VMEM(array.shape, bf16) for array in big]
         + [
             pltpu.VMEM((span, width), bf16),
@@ -329,7 +342,7 @@
             pltpu.SemaphoreType.DMA((3, parts)),
         ],
         compiler_params=pltpu.CompilerParams(
-            collective_id=0, has_side_effects=True, vmem_limit_bytes=56 * 2**20
+            collective_id=0, has_side_effects=True, vmem_limit_bytes=58 * 2**20
         ),
         cost_estimate=pl.CostEstimate(flops=4 * size, bytes_accessed=2 * size, transcendentals=0),
     )(
@@ -342,6 +355,13 @@
         gain_final.reshape(1, depth),
         *big,
     )
+    return pl.pallas_call(
+        hand_over,
+        out_shape=tuple(jax.ShapeDtypeStruct(array.shape, array.dtype) for array in results),
+        in_specs=[anywhere] * len(results),
+        out_specs=(anywhere,) * len(results),
+        scratch_shapes=[pltpu.SemaphoreType.DMA((len(results),))],
+    )(*(pltpu.with_memory_space_constraint(array, pltpu.VMEM) for array in results))
 
 
 def solution(mesh):

time: 62.1 us -> 54.9 us (0.88)
  local copies, waits for them, and re-layouts: 7.49 us -> 0 us
    unnamed x5 -> x0, local copies, waits for them, and re-layouts: 7.49 us -> none
    pallas_call x1 -> x2, Pallas kernels: 53 us -> 53.4 us  [the longest x1 52.4 us: on_device(): pl.pallas_call(functools.partial(kernel, parts, places), out_shape=(pltpu...]
where the time goes in v3:
time: 54.9 us; the launch traced here: 54.7 us
  Pallas kernels  53.4 us (97%)
  between operations  1.29 us (2%)
    pallas_call x1, Pallas kernels, on_device(): pl.pallas_call(functools.partial(kernel, parts, places), out_shape=(pltpu...  52.4 us

profile of v3, /device:TPU:0, one launch (start us, length us, event | category | flops | bytes accessed | tf_op | source)
XLA Modules:
  0.0 54.7 jit_solution(4421452313412736783)
XLA Ops:
  1.3 52.4 %shard_map.218 = (bf16[2,1024]{1,0:T(2,128)(2,1)S(1)}, bf16[2,512]{1,0:T(2,128)(2,1)S(1)}, bf16[2,512]{1,0:T(2,128)(2,1)S(1)}, bf16[1,512,512]{2,1,0:T(8,128)(2,1)S(1)}, bf16[1,512,512]{2,1,0:T(8,128)(2,1)S(1)}) custom-call(s32[2]{0:T(128)} %self_len.1, s32[2]{0:T(128)} %cross_len.1, s32[1]{0:T(128)S(6)} %copy.24.give_slot, bf16[2,1024]{1,0:T(2,128)(2,1)} %tokens.1, ...), custom_call_target="tpu_custom_call" | custom-call | flops 37748736 | bytes 18874368 | tf_op jit(solution)/shard_map/pallas_call | solution.py:318
  53.7 1.0 %shard_map.219 = (bf16[2,1024]{1,0:T(2,128)(2,1)}, bf16[2,512]{1,0:T(2,128)(2,1)}, bf16[2,512]{1,0:T(2,128)(2,1)}, bf16[1,512,512]{2,1,0:T(8,128)(2,1)}, bf16[1,512,512]{2,1,0:T(8,128)(2,1)}) custom-call(bf16[2,1024]{1,0:T(2,128)(2,1)S(1)} %get-tuple-element.10.refs_0_, bf16[2,512]{1,0:T(2,128)(2,1)S(1)} %get-tuple-element.11.refs_1_, ...), custom_call_target="tpu_custom_call" | custom-call | tf_op jit(solution)/shard_map/pallas_call | solution.py:358

commit v4 on v3

--- a/solution.py
+++ b/solution.py
@@ -59,13 +59,13 @@
 def kernel(
     parts,
     places,
-    self_len,
-    cross_len,
-    give_slot,
-    tokens,
-    gain_self,
-    gain_cross,
-    gain_final,
+    self_len_out,
+    cross_len_out,
+    give_slot_out,
+    tokens_out,
+    gain_self_out,
+    gain_cross_out,
+    gain_final_out,
     self_keys,
     self_values,
     cross_keys,
@@ -95,6 +95,13 @@
     cross_out_in,
     up_in,
     down_in,
+    self_len,
+    cross_len,
+    give_slot,
+    tokens,
+    gain_self,
+    gain_cross,
+    gain_final,
     keys_away,
     values_away,
     hold,
@@ -113,6 +120,11 @@
     partner = lax.rem(place + places // 2, places)
     peers = [lax.rem(part + step, parts) for step in range(1, parts)]
 
+    barrier = pltpu.get_barrier_semaphore()
+    pl.semaphore_signal(barrier, inc=1, device_id=(partner, part), device_id_type=MESH)
+    for peer in peers:
+        pl.semaphore_signal(barrier, inc=1, device_id=(place, peer), device_id_type=MESH)
+
     loads = []
     for index, (source, target) in enumerate(
         (
@@ -128,17 +140,21 @@
             (w_cross_out, cross_out_in),
             (w_up, up_in),
             (w_down, down_in),
+            (give_slot_out, give_slot),
+            (tokens_out, tokens),
+            (self_len_out, self_len),
+            (cross_len_out, cross_len),
+            (gain_self_out, gain_self),
+            (gain_cross_out, gain_cross),
+            (gain_final_out, gain_final),
         )
     ):
         load = pltpu.make_async_copy(source, target, load_sem.at[index])
-        load.start()
         loads.append(load)
-
-    barrier = pltpu.get_barrier_semaphore()
-    pl.semaphore_signal(barrier, inc=1, device_id=(partner, part), device_id_type=MESH)
-    for peer in peers:
-        pl.semaphore_signal(barrier, inc=1, device_id=(place, peer), device_id_type=MESH)
-
+    for index in (0, 12, 1, 13, 2, 3, 4, 14, 5, 16, 6, 7, 15, 8, 9, 17, 10, 11, 18):
+        loads[index].start()
+
+    loads[12].wait()
     chosen = give_slot[0]
     first_chosen = chosen == 0
 
@@ -186,6 +202,8 @@
 
     count = tokens.shape[0]
     scale = HEAD_DIM ** (-0.5)
+    for index in range(13, 19):
+        loads[index].wait()
     hold[...] = jnp.zeros_like(hold)
     hold[0:count, :] = tokens[...].astype(jnp.float32)
     own = hold[...]
@@ -311,7 +329,6 @@
         w_down,
     )
     whole = pl.BlockSpec(memory_space=pltpu.VMEM)
-    scalars = pl.BlockSpec(memory_space=pltpu.SMEM)
     anywhere = pl.BlockSpec(memory_space=pl.ANY)
     bf16, f32 = jnp.bfloat16, jnp.float32
     size = sum(array.size for array in big)
@@ -324,10 +341,17 @@
             pltpu.VMEM((1, span, width), bf16),
             pltpu.VMEM((1, span, width), bf16),
         ),
-        in_specs=[scalars] * 3 + [whole] * 4 + [anywhere] * 12,
+        in_specs=[anywhere] * 19,
         out_specs=(whole,) * 5,
         scratch_shapes=[pltpu.VMEM(array.shape, bf16) for array in big]
         + [
+            pltpu.SMEM(self_len.shape, self_len.dtype),
+            pltpu.SMEM(cross_len.shape, cross_len.dtype),
+            pltpu.SMEM(give_slot.shape, give_slot.dtype),
+            pltpu.VMEM(tokens.shape, bf16),
+            pltpu.VMEM((1, depth), f32),
+            pltpu.VMEM((1, depth), f32),
+            pltpu.VMEM((1, depth), f32),
             pltpu.VMEM((span, width), bf16),
             pltpu.VMEM((span, width), bf16),
             pltpu.VMEM((ROWS, depth), f32),
@@ -335,7 +359,7 @@
             pltpu.VMEM((3, parts, ROWS, depth), f32),
             pltpu.VMEM((tall, LANES), f32),
             pltpu.VMEM((tall, LANES), f32),
-            pltpu.SemaphoreType.DMA((len(big),)),
+            pltpu.SemaphoreType.DMA((len(big) + 7,)),
             pltpu.SemaphoreType.DMA((3,)),
             pltpu.SemaphoreType.DMA((3,)),
             pltpu.SemaphoreType.DMA((3, parts)),

time: 54.9 us -> 54.1 us (0.985)
  Pallas kernels: 53.4 us -> 52.7 us
    pallas_call x1, Pallas kernels: 52.4 us -> 51.7 us  [on_device(): pl.pallas_call(functools.partial(kernel, parts, places), out_shape=(pltpu...]
where the time goes in v4:
time: 54.1 us; the launch traced here: 54 us
  Pallas kernels  52.7 us (97%)
  between operations  1.29 us (2%)
    pallas_call x1, Pallas kernels, on_device(): pl.pallas_call(functools.partial(kernel, parts, places), out_shape=(pltpu...  51.7 us

profile of v4, /device:TPU:0, one launch (start us, length us, event | category | flops | bytes accessed | tf_op | source)
XLA Modules:
  0.0 54.0 jit_solution(16569694319537267766)
XLA Ops:
  1.3 51.7 %shard_map.218 = (bf16[2,1024]{1,0:T(2,128)(2,1)S(1)}, bf16[2,512]{1,0:T(2,128)(2,1)S(1)}, bf16[2,512]{1,0:T(2,128)(2,1)S(1)}, bf16[1,512,512]{2,1,0:T(8,128)(2,1)S(1)}, bf16[1,512,512]{2,1,0:T(8,128)(2,1)S(1)}) custom-call(s32[2]{0:T(128)} %self_len_out.1, s32[2]{0:T(128)} %cross_len_out.1, s32[1]{0:T(128)S(6)} %copy.24.give_slot_out, ...), custom_call_target="tpu_custom_call" | custom-call | flops 37748736 | bytes 18874368 | tf_op jit(solution)/shard_map/pallas_call | solution.py:335
  53.0 1.0 %shard_map.219 = (bf16[2,1024]{1,0:T(2,128)(2,1)}, bf16[2,512]{1,0:T(2,128)(2,1)}, bf16[2,512]{1,0:T(2,128)(2,1)}, bf16[1,512,512]{2,1,0:T(8,128)(2,1)}, bf16[1,512,512]{2,1,0:T(8,128)(2,1)}) custom-call(bf16[2,1024]{1,0:T(2,128)(2,1)S(1)} %get-tuple-element.10.refs_0_, bf16[2,512]{1,0:T(2,128)(2,1)S(1)} %get-tuple-element.11.refs_1_, ...), custom_call_target="tpu_custom_call" | custom-call | tf_op jit(solution)/shard_map/pallas_call | solution.py:382
